TPU v7x, 32 devices: a whole 2x2x4 slice. The times are simulated.
32 devices in a mesh: rep: 16 (over z, x, core), shard: 2 (over y).
Axes of the slice: x: 2, y: 2, z: 4, core: 2. Of those that a mesh axis runs over, the one named last changes fastest.
Arguments:
- images: bfloat16 [32, 577, 1024], P(('rep', 'shard')), may hold values from -6 to 6
- qkv_weight: bfloat16 [1024, 3072], P('shard'), may hold values from -0.1875 to 0.1875
- out_weight: bfloat16 [1024, 1024], P('shard'), may hold values from -2 to 2
- up_weight: bfloat16 [1024, 4096], P('shard'), may hold values from -0.1875 to 0.1875
- down_weight: bfloat16 [4096, 1024], P('shard'), may hold values from -0.09375 to 0.09375
- query_bias: bfloat16 [1024], P('shard'), may hold values from -1.796875 to 1.796875
- value_bias: bfloat16 [1024], P('shard'), may hold values from -1.796875 to 1.796875
- out_bias: bfloat16 [1024], P('shard'), may hold values from -1.796875 to 1.796875
- up_bias: bfloat16 [4096], P('shard'), may hold values from -1.796875 to 1.796875
- down_bias: bfloat16 [1024], P('shard'), may hold values from -1.796875 to 1.796875
- first_gain: bfloat16 [1024], P('shard'), may hold values from 0.5 to 1.5
- first_shift: bfloat16 [1024], P('shard'), may hold values from -1.796875 to 1.796875
- second_gain: bfloat16 [1024], P('shard'), may hold values from 0.5 to 1.5
- second_shift: bfloat16 [1024], P('shard'), may hold values from -1.796875 to 1.796875
- cotangent: bfloat16 [32, 577, 1024], P(('rep', 'shard')), may hold values from -6 to 6
Outputs:
- output: bfloat16 [32, 577, 1024], P(('rep', 'shard'))
- input_grad: float32 [32, 577, 1024], P(('rep', 'shard'))
- qkv_grad: float32 [1024, 3072], P('shard')
- out_grad: float32 [1024, 1024], P('shard')
- up_grad: float32 [1024, 4096], P('shard')
- down_grad: float32 [4096, 1024], P('shard')
- query_bias_grad: float32 [1024], P('shard')
- value_bias_grad: float32 [1024], P('shard')
- out_bias_grad: float32 [1024], P('shard')
- up_bias_grad: float32 [4096], P('shard')
- down_bias_grad: float32 [1024], P('shard')
- first_gain_grad: float32 [1024], P('shard')
- first_shift_grad: float32 [1024], P('shard')
- second_gain_grad: float32 [1024], P('shard')
- second_shift_grad: float32 [1024], P('shard')
All inputs are finite; a program needn't handle non-finite values.
Results may differ from a plain program's by a relative error of at most 0.01.
Values may be sent and summed in bfloat16 or wider, within the bound.
No kernel may reach another device: no remote copies, remote signals or barrier semaphores. Data moves between devices by JAX's collectives and lax.ppermute only.
A program may use at most 256 MiB of HBM per device.

v0:
```python
import jax
import jax.numpy as jnp
from jax import lax
from jax.sharding import PartitionSpec as P

HEADS = 16
HEAD_DIM = 64


def normalize(value, gain, shift):
    center = value - jnp.mean(value, -1, keepdims=True)
    spread = jnp.mean(center * center, -1, keepdims=True)
    return center * lax.rsqrt(spread + 1e-06) * gain + shift


def exact_gelu(value):
    return jax.nn.gelu(value, approximate=False)


def attend_forward(item):
    query, key, value = item
    scores = jnp.einsum("qhe,khe->hqk", query, key, preferred_element_type=jnp.float32) * 0.125
    largest = jnp.max(scores, -1, keepdims=True)
    shifted = jnp.exp(scores - largest)
    total = jnp.sum(shifted, -1, keepdims=True)
    probs = (shifted / total).astype(jnp.bfloat16)
    mixed = jnp.einsum("hqk,khe->qhe", probs, value, preferred_element_type=jnp.float32)
    return (mixed, largest + jnp.log(total))


def attend_backward(item):
    query, key, value, logsum, grad_mixed = item
    scores = jnp.einsum("qhe,khe->hqk", query, key, preferred_element_type=jnp.float32) * 0.125
    probs = jnp.exp(scores - logsum)
    grad_value = jnp.einsum(
        "hqk,qhe->khe", probs.astype(jnp.bfloat16), grad_mixed, preferred_element_type=jnp.float32
    )
    grad_probs = jnp.einsum("qhe,khe->hqk", grad_mixed, value, preferred_element_type=jnp.float32)
    grad_scores = probs * (grad_probs - jnp.sum(grad_probs * probs, -1, keepdims=True))
    grad_scores = grad_scores.astype(jnp.bfloat16)
    grad_query = (
        jnp.einsum("hqk,khe->qhe", grad_scores, key, preferred_element_type=jnp.float32) * 0.125
    )
    grad_key = (
        jnp.einsum("hqk,qhe->khe", grad_scores, query, preferred_element_type=jnp.float32) * 0.125
    )
    return (grad_query, grad_key, grad_value)


def body(
    images,
    qkv_weight,
    out_weight,
    up_weight,
    down_weight,
    query_bias,
    value_bias,
    out_bias,
    up_bias,
    down_bias,
    first_gain,
    first_shift,
    second_gain,
    second_shift,
    cotangent,
):
    (
        qkv_full,
        out_full,
        up_full,
        down_full,
        query_full,
        value_full,
        outb_full,
        upb_full,
        downb_full,
        gain_one,
        shift_one,
        gain_two,
        shift_two,
    ) = (
        lax.all_gather(qkv_weight, "shard", axis=0, tiled=True),
        lax.all_gather(out_weight, "shard", axis=0, tiled=True),
        lax.all_gather(up_weight, "shard", axis=0, tiled=True),
        lax.all_gather(down_weight, "shard", axis=0, tiled=True),
        lax.all_gather(query_bias, "shard", axis=0, tiled=True),
        lax.all_gather(value_bias, "shard", axis=0, tiled=True),
        lax.all_gather(out_bias, "shard", axis=0, tiled=True),
        lax.all_gather(up_bias, "shard", axis=0, tiled=True),
        lax.all_gather(down_bias, "shard", axis=0, tiled=True),
        lax.all_gather(first_gain, "shard", axis=0, tiled=True),
        lax.all_gather(first_shift, "shard", axis=0, tiled=True),
        lax.all_gather(second_gain, "shard", axis=0, tiled=True),
        lax.all_gather(second_shift, "shard", axis=0, tiled=True),
    )
    batch, length, width = images.shape
    tokens = images.astype(jnp.float32)
    gain_one = gain_one.astype(jnp.float32)
    shift_one = shift_one.astype(jnp.float32)
    gain_two = gain_two.astype(jnp.float32)
    shift_two = shift_two.astype(jnp.float32)
    first = normalize(tokens, gain_one, shift_one).astype(jnp.bfloat16)
    joined = jnp.einsum("bsd,de->bse", first, qkv_full, preferred_element_type=jnp.float32)
    joined = joined + jnp.concatenate(
        [
            query_full.astype(jnp.float32),
            jnp.zeros((width,), jnp.float32),
            value_full.astype(jnp.float32),
        ]
    )
    joined = joined.astype(jnp.bfloat16)
    query = joined[..., :width].reshape(batch, length, HEADS, HEAD_DIM)
    key = joined[..., width : 2 * width].reshape(batch, length, HEADS, HEAD_DIM)
    value = joined[..., 2 * width :].reshape(batch, length, HEADS, HEAD_DIM)
    mixed, logsum = lax.map(attend_forward, (query, key, value))
    mixed = mixed.reshape(batch, length, width).astype(jnp.bfloat16)
    resid = (
        tokens
        + jnp.einsum("bsd,de->bse", mixed, out_full, preferred_element_type=jnp.float32)
        + outb_full.astype(jnp.float32)
    )
    second = normalize(resid, gain_two, shift_two).astype(jnp.bfloat16)
    hidden = jnp.einsum(
        "bsd,df->bsf", second, up_full, preferred_element_type=jnp.float32
    ) + upb_full.astype(jnp.float32)
    active = exact_gelu(hidden).astype(jnp.bfloat16)
    result = (
        resid
        + jnp.einsum("bsf,fd->bsd", active, down_full, preferred_element_type=jnp.float32)
        + downb_full.astype(jnp.float32)
    )
    output = result.astype(jnp.bfloat16)
    (
        qkv_back,
        out_back,
        up_back,
        down_back,
        unused_query,
        unused_value,
        unused_outb,
        unused_upb,
        unused_downb,
        unused_gain1,
        unused_shift1,
        unused_gain2,
        unused_shift2,
    ) = (
        lax.all_gather(qkv_weight, "shard", axis=0, tiled=True),
        lax.all_gather(out_weight, "shard", axis=0, tiled=True),
        lax.all_gather(up_weight, "shard", axis=0, tiled=True),
        lax.all_gather(down_weight, "shard", axis=0, tiled=True),
        lax.all_gather(query_bias, "shard", axis=0, tiled=True),
        lax.all_gather(value_bias, "shard", axis=0, tiled=True),
        lax.all_gather(out_bias, "shard", axis=0, tiled=True),
        lax.all_gather(up_bias, "shard", axis=0, tiled=True),
        lax.all_gather(down_bias, "shard", axis=0, tiled=True),
        lax.all_gather(first_gain, "shard", axis=0, tiled=True),
        lax.all_gather(first_shift, "shard", axis=0, tiled=True),
        lax.all_gather(second_gain, "shard", axis=0, tiled=True),
        lax.all_gather(second_shift, "shard", axis=0, tiled=True),
    )
    grad_out = cotangent.astype(jnp.float32)
    down_local = jnp.einsum("bsf,bsd->fd", active, cotangent, preferred_element_type=jnp.float32)
    downb_local = jnp.sum(grad_out, (0, 1))
    grad_active = jnp.einsum(
        "bsd,fd->bsf", cotangent, down_back, preferred_element_type=jnp.float32
    )
    unused_gelu, gelu_back = jax.vjp(exact_gelu, hidden)
    grad_hidden = gelu_back(grad_active)[0].astype(jnp.bfloat16)
    up_local = jnp.einsum("bsd,bsf->df", second, grad_hidden, preferred_element_type=jnp.float32)
    upb_local = jnp.sum(grad_hidden.astype(jnp.float32), (0, 1))
    grad_second = jnp.einsum(
        "bsf,df->bsd", grad_hidden, up_back, preferred_element_type=jnp.float32
    )
    unused_norm2, norm_back2 = jax.vjp(normalize, resid, gain_two, shift_two)
    grad_resid, gain2_local, shift2_local = norm_back2(grad_second)
    grad_resid = grad_out + grad_resid
    grad_attn = grad_resid.astype(jnp.bfloat16)
    out_local = jnp.einsum("bsd,bse->de", mixed, grad_attn, preferred_element_type=jnp.float32)
    outb_local = jnp.sum(grad_attn.astype(jnp.float32), (0, 1))
    grad_mixed = jnp.einsum("bse,de->bsd", grad_attn, out_back, preferred_element_type=jnp.float32)
    grad_mixed = grad_mixed.astype(jnp.bfloat16).reshape(batch, length, HEADS, HEAD_DIM)
    grad_query, grad_key, grad_value = lax.map(
        attend_backward, (query, key, value, logsum, grad_mixed)
    )
    grad_joined = jnp.concatenate(
        [
            grad_query.reshape(batch, length, width),
            grad_key.reshape(batch, length, width),
            grad_value.reshape(batch, length, width),
        ],
        -1,
    )
    grad_joined = grad_joined.astype(jnp.bfloat16)
    qkv_local = jnp.einsum("bsd,bse->de", first, grad_joined, preferred_element_type=jnp.float32)
    bias_sums = jnp.sum(grad_joined.astype(jnp.float32), (0, 1))
    query_local = bias_sums[:width]
    value_local = bias_sums[2 * width :]
    grad_first = jnp.einsum(
        "bse,de->bsd", grad_joined, qkv_back, preferred_element_type=jnp.float32
    )
    unused_norm1, norm_back1 = jax.vjp(normalize, tokens, gain_one, shift_one)
    grad_tokens, gain1_local, shift1_local = norm_back1(grad_first)
    input_grad = grad_resid + grad_tokens
    owned = (
        lax.psum_scatter(qkv_local, "shard", scatter_dimension=0, tiled=True),
        lax.psum_scatter(out_local, "shard", scatter_dimension=0, tiled=True),
        lax.psum_scatter(up_local, "shard", scatter_dimension=0, tiled=True),
        lax.psum_scatter(down_local, "shard", scatter_dimension=0, tiled=True),
        lax.psum_scatter(query_local, "shard", scatter_dimension=0, tiled=True),
        lax.psum_scatter(value_local, "shard", scatter_dimension=0, tiled=True),
        lax.psum_scatter(outb_local, "shard", scatter_dimension=0, tiled=True),
        lax.psum_scatter(upb_local, "shard", scatter_dimension=0, tiled=True),
        lax.psum_scatter(downb_local, "shard", scatter_dimension=0, tiled=True),
        lax.psum_scatter(gain1_local, "shard", scatter_dimension=0, tiled=True),
        lax.psum_scatter(shift1_local, "shard", scatter_dimension=0, tiled=True),
        lax.psum_scatter(gain2_local, "shard", scatter_dimension=0, tiled=True),
        lax.psum_scatter(shift2_local, "shard", scatter_dimension=0, tiled=True),
    )
    (
        qkv_grad,
        out_grad,
        up_grad,
        down_grad,
        query_bias_grad,
        value_bias_grad,
        out_bias_grad,
        up_bias_grad,
        down_bias_grad,
        first_gain_grad,
        first_shift_grad,
        second_gain_grad,
        second_shift_grad,
    ) = lax.psum(
        (
            owned[0],
            owned[1],
            owned[2],
            owned[3],
            owned[4],
            owned[5],
            owned[6],
            owned[7],
            owned[8],
            owned[9],
            owned[10],
            owned[11],
            owned[12],
        ),
        "rep",
    )
    return (
        output,
        input_grad,
        qkv_grad,
        out_grad,
        up_grad,
        down_grad,
        query_bias_grad,
        value_bias_grad,
        out_bias_grad,
        up_bias_grad,
        down_bias_grad,
        first_gain_grad,
        first_shift_grad,
        second_gain_grad,
        second_shift_grad,
    )


def solution(mesh):
    return jax.shard_map(
        body,
        mesh=mesh,
        in_specs=(
            P(("rep", "shard"), None, None),
            P("shard", None),
            P("shard", None),
            P("shard", None),
            P("shard", None),
            P("shard"),
            P("shard"),
            P("shard"),
            P("shard"),
            P("shard"),
            P("shard"),
            P("shard"),
            P("shard"),
            P("shard"),
            P(("rep", "shard"), None, None),
        ),
        out_specs=(
            P(("rep", "shard"), None, None),
            P(("rep", "shard"), None, None),
            P("shard", None),
            P("shard", None),
            P("shard", None),
            P("shard", None),
            P("shard"),
            P("shard"),
            P("shard"),
            P("shard"),
            P("shard"),
            P("shard"),
            P("shard"),
            P("shard"),
            P("shard"),
        ),
        check_vma=False,
    )
```

profile of v0, /device:TPU:0, one launch (start us, length us, event | category | flops | bytes accessed | tf_op | source)
XLA Modules:
  0.0 1460.8 jit_solution(5654971569421349332)
XLA Ops:
  10.1 5.3 all-gather.4
  15.4 4.3 all-gather.3
  19.8 4.3 all-gather.2
  24.1 4.4 all-gather.1
  28.5 4.4 all-gather
  33.7 4.4 all_gather.53
  38.1 4.4 all-gather.6
  42.5 4.4 all-gather.5
  46.9 46.1 %all-gather.13.cloned.1.call-done = bf16[1024,3072]{1,0:T(8,128)(2,1)} async-done(((bf16[512,3072]{1,0:T(8,128)(2,1)}), bf16[1024,3072]{1,0:T(8,128)(2,1)}) %all-gather.13.cloned.1.call-update) | async-done | bytes 6291472 | tf_op jit(solution)/shard_map/all_gather | solution.py:82
  92.9 7.4 fusion.13
  106.3 13.7 multiply_reduce_fusion.1
  120.0 10.5 fusion
  130.5 13.5 fusion.35
  143.9 4.4 fusion.66
  148.7 84.5 %all-gather.17.cloned.1.call-done = bf16[1024,4096]{1,0:T(8,128)(2,1)} async-done(((bf16[512,4096]{1,0:T(8,128)(2,1)}), bf16[1024,4096]{1,0:T(8,128)(2,1)}) %all-gather.17.cloned.1.call-update) | async-done | bytes 8388624 | tf_op jit(solution)/shard_map/all_gather | solution.py:84
  233.2 31.4 %multiply_convert_fusion.1 = (bf16[577,4096]{1,0:T(8,128)(2,1)}, f32[577,4096]{1,0:T(8,128)}, f32[577,4096]{1,0:T(8,128)}) fusion(f32[4096]{0:T(1024)S(1)} %convert_element_type.136, bf16[1024,4096]{1,0:T(8,128)(2,1)} %all-gather.17.cloned.1.call-done, f32[1,577,1024]{2,1,0:T(8,128)S(1)} %get-tuple-element.147, f32[1024]{0:T(1024)S(1)} %bitcast.133, ...), kind=kOutput, calls=%fused_computation.16 | convolution fusion | flops 4999164928 | bytes 34415112 | tf_op jit(solution)/shard_map/bsd,df->bsf/dot_general | solution.py:123
  264.7 74.0 %all-gather.19.cloned.1.call-done = bf16[4096,1024]{1,0:T(8,128)(2,1)} async-done(((bf16[2048,1024]{1,0:T(8,128)(2,1)}), bf16[4096,1024]{1,0:T(8,128)(2,1)}) %all-gather.19.cloned.1.call-update) | async-done | bytes 8388624 | tf_op jit(solution)/shard_map/all_gather | solution.py:85
  338.7 15.1 %convert_reduce_fusion = (f32[4096]{0:T(1024)S(1)}, bf16[577,4096]{1,0:T(8,128)(2,1)S(1)}) fusion(f32[577,4096]{1,0:T(8,128)} %get-tuple-element.136, bf16[4096,1024]{1,0:T(8,128)(2,1)} %all-gather.19.cloned.1.call-done, bf16[1,577,1024]{2,1,0:T(8,128)(2,1)} %param.29, f32[577,4096]{1,0:T(8,128)} %get-tuple-element.148, f32[4096]{0:T(1024)S(1)} %convert_element_type.136), kind=kOutput, calls=%fused_computation.14 | convolution fusion | flops 4880400384 | bytes 33236992 | tf_op jit(solution)/shard_map/bsd,fd->bsf/dot_general | solution.py:165
  353.8 9.7 fusion.26
  367.3 3.8 fusion.39
  371.2 4.5 convolution_convert_fusion
  375.6 2.4 copy.56
  378.1 16.0 %multiply_reduce_fusion = (f32[16,577]{1,0:T(8,128)S(1)}, f32[16,577,577]{1,2,0:T(8,128)}) fusion(f32[16,577,577]{1,2,0:T(8,128)} %get-tuple-element.145, f32[16,577]{1,0:T(8,128)S(1)} %log_add_fusion, bf16[577,16,64]{0,2,1:T(8,128)(2,1)} %bitcast.112, bf16[577,16,64]{0,2,1:T(8,128)(2,1)} %bitcast.124), kind=kOutput, calls=%fused_computation.1 | convolution fusion | flops 703136768 | bytes 45052160 | tf_op jit(solution)/shard_map/while/body/eval_jaxpr/qhe,khe->hqk/dot_general | solution.py:38
  394.0 20.8 %multiply_convert_fusion = bf16[16,577,577]{1,2,0:T(8,128)(2,1)} fusion(f32[16,577,577]{1,2,0:T(8,128)} %get-tuple-element.151, f32[16,577,577]{1,2,0:T(8,128)} %get-tuple-element.145, f32[16,577]{1,0:T(8,128)S(1)} %get-tuple-element.150, f32[16,577]{1,0:T(8,128)S(1)} %log_add_fusion), kind=kLoop, calls=%fused_computation | loop fusion | flops 26634320 | bytes 53342496 | tf_op jit(solution)/shard_map/while/body/eval_jaxpr/convert_element_type | solution.py:40
  414.8 9.2 multiply_convert_fusion.2
  424.0 7.8 multiply_convert_fusion.3
  431.8 13.4 fusion.32
  445.3 12.8 fusion.30
  458.1 13.0 fusion.57
  471.2 12.4 fusion.42
  483.7 120.1 %reduce-scatter.5.cloned.1.call-done = f32[512,3072]{1,0:T(8,128)} async-done(((f32[1024,3072]{1,0:T(8,128)}), f32[512,3072]{1,0:T(8,128)}) %reduce-scatter.5.cloned.1.call-update) | async-done | bytes 6291472 | tf_op jit(solution)/shard_map/reduce_scatter | solution.py:206
  603.8 191.5 %reduce-scatter.9.cloned.1.call-done = f32[512,4096]{1,0:T(8,128)} async-done(((f32[1024,4096]{1,0:T(8,128)}), f32[512,4096]{1,0:T(8,128)}) %reduce-scatter.9.cloned.1.call-update) | async-done | bytes 8388624 | tf_op jit(solution)/shard_map/reduce_scatter | solution.py:208
  795.4 191.5 %reduce-scatter.11.cloned.1.call-done = f32[2048,1024]{1,0:T(8,128)} async-done(((f32[4096,1024]{1,0:T(8,128)}), f32[2048,1024]{1,0:T(8,128)}) %reduce-scatter.11.cloned.1.call-update) | async-done | bytes 8388624 | tf_op jit(solution)/shard_map/reduce_scatter | solution.py:209
  987.5 4.6 all-gather.7
  994.0 1.8 reduce_sum.192
  995.8 11.0 fusion.24
  1006.9 1.9 reduce_sum.190
  1008.9 3.3 fusion.22
  1012.2 2.9 convert_reduce_fusion.3
  1015.1 3.8 copy.60
  1019.0 4.0 convert_reduce_fusion.1
  1023.0 7.2 all-reduce.11
  1030.8 62.4 %all-reduce.9 = (f32[512]{0:T(512)}, f32[512]{0:T(512)}, f32[512]{0:T(512)}, f32[2048]{0:T(1024)}, f32[512]{0:T(512)}, /*index=5*/f32[512]{0:T(512)}, f32[512]{0:T(512)}, f32[512]{0:T(512)}, f32[512]{0:T(512)}) all-reduce(f32[512]{0:T(512)S(1)} %dynamic-slice.2, ...), channel_id=1, replica_groups=mesh['rep'=16,'shard'=2] {'rep'}, use_global_device_ids=true, to_apply=%region_21.22 | all-reduce | flops 6144 | bytes 49152 | tf_op jit(solution)/shard_map/psum | solution.py:234
  1093.2 9.9 fusion.29
  1103.1 332.8 %all-reduce.14.cloned.1.call-done = (f32[512,3072]{1,0:T(8,128)}, f32[512,1024]{1,0:T(8,128)}, f32[512,4096]{1,0:T(8,128)}, f32[2048,1024]{1,0:T(8,128)}) async-done(((f32[512,3072]{1,0:T(8,128)}, f32[512,1024]{1,0:T(8,128)}, f32[512,4096]{1,0:T(8,128)}, f32[2048,1024]{1,0:T(8,128)}), (f32[512,3072]{1,0:T(8,128)}, f32[512,1024]{1,0:T(8,128)}, f32[512,4096]{1,0:T(8,128)}, ...) | async-done | bytes 25165840 | tf_op jit(solution)/shard_map/psum | solution.py:234
  1436.0 6.9 copy.69
  1444.6 4.3 copy.71
  1450.4 3.4 copy.72
  (150 shorter events, 19.1 us)
Async XLA Ops:
  7.2 85.7 %all-gather.13.cloned.1.call-start = ((), (), s32[]{:S(2)}) async-start(), calls=%async_computation.4 | async-start | bytes 9437184 | tf_op jit(solution)/shard_map/all_gather | solution.py:82
  7.9 136.0 %all-gather.15.cloned.1.call-start = ((), (), s32[]{:S(2)}) async-start(), calls=%async_computation.5 | async-start | bytes 3145728 | tf_op jit(solution)/shard_map/all_gather | solution.py:83
  8.7 1.5 copy-start.28
  8.7 6.7 copy-start.29
  8.7 11.1 copy-start.30
  8.7 15.4 %copy-start.31 = (bf16[512]{0:T(512)(128)(2,1)S(1)}, bf16[512]{0:T(512)(128)(2,1)}, u32[]{:S(2)}) copy-start(bf16[512]{0:T(512)(128)(2,1)} %param.26) | copy-start | bytes 3076
  8.7 19.8 %copy-start.32 = (bf16[512]{0:T(512)(128)(2,1)S(1)}, bf16[512]{0:T(512)(128)(2,1)}, u32[]{:S(2)}) copy-start(bf16[512]{0:T(512)(128)(2,1)} %param.25) | copy-start | bytes 3076
  8.7 24.2 %copy-start.2 = (bf16[1,577,1024]{2,1,0:T(8,128)(2,1)S(1)}, bf16[1,577,1024]{2,1,0:T(8,128)(2,1)}, u32[]{:S(2)}) copy-start(bf16[1,577,1024]{2,1,0:T(8,128)(2,1)} %param.15) | copy-start | bytes 3545092
  8.7 224.5 %all-gather.17.cloned.1.call-start = ((), (), s32[]{:S(2)}) async-start(), calls=%async_computation.6 | async-start | bytes 12582912 | tf_op jit(solution)/shard_map/all_gather | solution.py:84
  9.5 24.2 %copy-start.25 = (bf16[2048]{0:T(1024)(128)(2,1)S(1)}, bf16[2048]{0:T(1024)(128)(2,1)}, u32[]{:S(2)}) copy-start(bf16[2048]{0:T(1024)(128)(2,1)} %param.23) | copy-start | bytes 12292
  9.5 28.6 %copy-start.33 = (bf16[512]{0:T(512)(128)(2,1)S(1)}, bf16[512]{0:T(512)(128)(2,1)}, u32[]{:S(2)}) copy-start(bf16[512]{0:T(512)(128)(2,1)} %param.28) | copy-start | bytes 3076
  9.5 33.0 %copy-start.34 = (bf16[512]{0:T(512)(128)(2,1)S(1)}, bf16[512]{0:T(512)(128)(2,1)}, u32[]{:S(2)}) copy-start(bf16[512]{0:T(512)(128)(2,1)} %param.27) | copy-start | bytes 3076
  9.5 329.2 %all-gather.19.cloned.1.call-start = ((), (), s32[]{:S(2)}) async-start(), calls=%async_computation.7 | async-start | bytes 12582912 | tf_op jit(solution)/shard_map/all_gather | solution.py:85
  10.1 473.7 %reduce-scatter.7.cloned.1.call-start = ((), (), s32[]{:S(2)}) async-start(), calls=%async_computation.9 | async-start | bytes 6291456 | tf_op jit(solution)/shard_map/reduce_scatter | solution.py:207
  28.5 71.8 %copy-start.26 = (f32[2,1,512]{2,1,0:T(1,128)}, f32[2,1,512]{2,1,0:T(1,128)S(1)}, u32[]{:S(2)}) copy-start(f32[2,1,512]{2,1,0:T(1,128)S(1)} %convert_element_type.150) | copy-start | bytes 12292
  32.9 67.4 %copy-start.21 = (f32[2,1,512]{2,1,0:T(1,128)}, f32[2,1,512]{2,1,0:T(1,128)S(1)}, u32[]{:S(2)}) copy-start(f32[2,1,512]{2,1,0:T(1,128)S(1)} %convert_element_type.149) | copy-start | bytes 12292
  33.2 67.1 %copy-start.19 = (f32[577]{0:T(1024)}, f32[577]{0:T(1024)S(1)}, u32[]{:S(2)}) copy-start(f32[577]{0:T(1024)S(1)} %broadcast_multiply_fusion.1) | copy-start | bytes 6928
  33.6 59.3 %copy-start.23 = (f32[577]{0:T(1024)}, f32[577]{0:T(1024)S(1)}, u32[]{:S(2)}) copy-start(f32[577]{0:T(1024)S(1)} %fusion.23) | copy-start | bytes 6928
  33.7 66.6 %copy-start.17 = (f32[577]{0:T(1024)}, f32[577]{0:T(1024)S(1)}, u32[]{:S(2)}) copy-start(f32[577]{0:T(1024)S(1)} %fusion.48) | copy-start | bytes 6928
  106.3 13.7 copy-start.4
  119.9 10.5 copy-start.11
  353.8 9.7 copy-start.14
  363.5 2.7 copy-start.7
  363.5 2.3 copy-start.13
  364.4 1.4 copy-start
  364.4 2.9 copy-start.36
  366.2 1.0 copy-start.16
  371.1 232.8 %reduce-scatter.5.cloned.1.call-start = ((), (), s32[]{:S(2)}) async-start(), calls=%async_computation.8 | async-start | bytes 18874368 | tf_op jit(solution)/shard_map/reduce_scatter | solution.py:206
  394.0 20.8 %copy-start.6 = (bf16[1,577,1024]{1,2,0:T(8,128)(2,1)S(1)}, bf16[1,577,1024]{1,2,0:T(8,128)(2,1)}, u32[]{:S(2)}) copy-start(bf16[1,577,1024]{1,2,0:T(8,128)(2,1)} %copy.53) | copy-start | bytes 3545092
  414.8 9.2 copy-start.5
  431.8 13.4 copy-start.18
  431.8 13.4 copy-start.20
  431.8 13.4 copy-start.22
  431.8 13.4 copy-start.27
  458.1 337.3 %reduce-scatter.9.cloned.1.call-start = ((), (), s32[]{:S(2)}) async-start(), calls=%async_computation.10 | async-start | bytes 25165824 | tf_op jit(solution)/shard_map/reduce_scatter | solution.py:208
  471.2 515.6 %reduce-scatter.11.cloned.1.call-start = ((), (), s32[]{:S(2)}) async-start(), calls=%async_computation.11 | async-start | bytes 25165824 | tf_op jit(solution)/shard_map/reduce_scatter | solution.py:209
  483.7 952.3 %all-reduce.14.cloned.1.call-start = ((), (), s32[]{:S(2)}) async-start(), calls=%async_computation.12 | async-start | bytes 50331648 | tf_op jit(solution)/shard_map/psum | solution.py:234
  986.8 5.3 copy-start.37
  995.8 13.0 copy-start.24
  1008.8 3.4 copy-start.1
  1008.8 3.4 copy-start.3
  1015.1 3.9 copy-start.9
  1015.1 3.9 copy-start.10
  1015.1 3.9 copy-start.12
  1436.0 6.9 copy-start.15
  1436.0 8.6 copy-start.8
  1442.8 6.0 slice-start
  1444.6 5.8 slice-start.1
  (1 other events, 0.7 us)
Sparse Core Ops, SparseCore 0:
  9.6 83.3 all-gather.12
  94.5 33.1 all-gather.14
  129.2 103.9 all-gather.16
  234.6 103.9 all-gather.18
  371.2 54.3 reduce-scatter.6
  458.2 145.5 reduce-scatter.4
  606.2 189.0 reduce-scatter.8
  797.7 189.1 reduce-scatter.10
  992.5 443.4 all-reduce.13
where the time goes:
time: 1470 us; the launch traced here: 1460 us
  waiting for transfers between devices  1040 us (71%)
  matrix products  209 us (14%)
  blocking collectives  110 us (7%)
  other arithmetic  47.7 us (3%)
  local copies, waits for them, and re-layouts  34.4 us (2%)
  between operations  16.3 us (1%)
    psum x1, waiting for transfers between devices, body(): lax.psum((owned[0], owned[1], owned[2], owned[3], owned[4], owned[5], own...  333 us
    reduce_scatter x1, waiting for transfers between devices, body(): lax.psum_scatter(up_local, 'shard', scatter_dimension=0, tiled=True)  192 us
    reduce_scatter x1, waiting for transfers between devices, body(): lax.psum_scatter(down_local, 'shard', scatter_dimension=0, tiled=True)  191 us
    reduce_scatter x1, waiting for transfers between devices, body(): lax.psum_scatter(qkv_local, 'shard', scatter_dimension=0, tiled=True)  120 us
    all_gather x1, waiting for transfers between devices, body(): lax.all_gather(up_weight, 'shard', axis=0, tiled=True)  84.5 us
    all_gather x1, waiting for transfers between devices, body(): lax.all_gather(down_weight, 'shard', axis=0, tiled=True)  74 us
    psum x1, blocking collectives, body(): lax.psum((owned[0], owned[1], owned[2], owned[3], owned[4], owned[5], own...  62.4 us
    all_gather x1, waiting for transfers between devices, body(): lax.all_gather(qkv_weight, 'shard', axis=0, tiled=True)  46.1 us
  transfers between devices with their start and end apart: 9, of which 7 were waited for; matrix products, arithmetic and copies ran while one was open for 16% of the time, Pallas kernels for 0%

commit v1 on v0

v1 whole, which is shorter than its diff:
```python
import functools
import jax
import jax.numpy as jnp
from jax import lax
from jax.experimental import pallas as pl
from jax.experimental.pallas import tpu as pltpu
from jax.sharding import Mesh
from jax.sharding import PartitionSpec as P

LANES = 128
VMEM_LIMIT = 48 * 1024 * 1024


def round_up(value, multiple):
    return -(-value // multiple) * multiple


def slabs(length):
    top = round_up(length, 16)
    return [(low, min(LANES, top - low)) for low in range(0, top, LANES)]


def contract(left, right, left_dim, right_dim):
    return lax.dot_general(
        left, right, (((left_dim,), (right_dim,)), ((), ())), preferred_element_type=jnp.float32
    )


def clean(ref, length):
    rows = lax.broadcasted_iota(jnp.int32, ref.shape, 0)
    return jnp.where(rows < length, ref[...], jnp.zeros(ref.shape, ref.dtype))


def attend_kernel(length, query_ref, key_ref, value_ref, mixed_ref, logsum_ref):
    query = clean(query_ref, length) * jnp.bfloat16(0.125)
    key = clean(key_ref, length)
    value_turned = jnp.transpose(clean(value_ref, length))
    first = lax.broadcasted_iota(jnp.int32, query.shape, 1) < LANES // 2
    half = LANES // 2
    turned = []
    for head in range(2):
        own_query = jnp.where(first if head == 0 else ~first, query, jnp.zeros_like(query))
        scores, largest = [], None
        for low, size in slabs(length):
            part = contract(key[low : low + size], own_query, 1, 1)
            if low + size > length:
                rows = lax.broadcasted_iota(jnp.int32, part.shape, 0) + low
                part = jnp.where(rows < length, part, -1e30)
            scores.append(part)
            top = jnp.max(part, 0, keepdims=True)
            largest = top if largest is None else jnp.maximum(largest, top)
        total, mixed = None, None
        for (low, size), part in zip(slabs(length), scores):
            shifted = jnp.exp(part - largest)
            added = jnp.sum(shifted, 0, keepdims=True)
            weighted = contract(
                value_turned[head * half : (head + 1) * half, low : low + size],
                shifted.astype(jnp.bfloat16), 1, 0,
            )
            total = added if total is None else total + added
            mixed = weighted if mixed is None else mixed + weighted
        turned.append(mixed * (1.0 / total))
        logsum_ref[0, head : head + 1, :] = largest + jnp.log(total)
    mixed_ref[...] = jnp.transpose(jnp.concatenate(turned, 0)).astype(jnp.bfloat16)


def attend(joined):
    length, width = joined.shape[0], joined.shape[1] // 3
    pairs, padded = width // LANES, round_up(length, LANES)
    block = lambda shift: pl.BlockSpec((padded, LANES), lambda i: (0, i + shift))
    return pl.pallas_call(
        functools.partial(attend_kernel, length),
        grid=(pairs,),
        in_specs=[block(0), block(pairs), block(2 * pairs)],
        out_specs=[block(0), pl.BlockSpec((1, 2, padded), lambda i: (i, 0, 0))],
        out_shape=[
            jax.ShapeDtypeStruct((length, width), jnp.bfloat16),
            jax.ShapeDtypeStruct((pairs, 2, padded), jnp.float32),
        ],
        compiler_params=pltpu.CompilerParams(vmem_limit_bytes=VMEM_LIMIT),
        cost_estimate=pl.CostEstimate(
            flops=16 * padded * padded * width, bytes_accessed=8 * length * width,
            transcendentals=padded * padded * 16,
        ),
        name="attend",
    )(joined, joined, joined)


def attend_back_kernel(
    length, query_ref, key_ref, value_ref, mixed_ref, grad_ref, logsum_ref, out_ref
):
    padded = query_ref.shape[0]
    query = clean(query_ref, length) * jnp.bfloat16(0.125)
    key = clean(key_ref, length)
    value = clean(value_ref, length)
    grad = clean(grad_ref, length)
    first = lax.broadcasted_iota(jnp.int32, query.shape, 1) < LANES // 2
    weighed = jnp.transpose(grad.astype(jnp.float32) * clean(mixed_ref, length).astype(jnp.float32))
    key_turned = jnp.transpose(key)
    zero = jnp.zeros_like(query)
    half = LANES // 2
    turned = []
    done = {}
    for head in range(2):
        mask = first if head == 0 else ~first
        own_query = jnp.where(mask, query, zero)
        own_grad = jnp.where(mask, grad, zero)
        delta = jnp.sum(weighed[head * half : (head + 1) * half], 0, keepdims=True)
        level = logsum_ref[0, head : head + 1, :]
        total = None
        for low, size in slabs(length):
            scores = contract(key[low : low + size], own_query, 1, 1)
            probs = jnp.exp(scores - level)
            if low + size > length:
                rows = lax.broadcasted_iota(jnp.int32, probs.shape, 0) + low
                probs = jnp.where(rows < length, probs, 0.0)
            dots = contract(value[low : low + size], own_grad, 1, 1)
            grad_scores = (probs * (dots - delta)).astype(jnp.bfloat16)
            done[head, low] = (
                contract(grad_scores, query, 1, 0),
                contract(probs.astype(jnp.bfloat16), grad, 1, 0),
            )
            part = contract(key_turned[head * half : (head + 1) * half, low : low + size], grad_scores, 1, 0)
            total = part if total is None else total + part
            if head == 1:
                side = lax.broadcasted_iota(jnp.int32, (size, LANES), 1) < half
                one, two = done[0, low], done[1, low]
                out_ref[1, low : low + size, :] = jnp.where(side, one[0], two[0]).astype(jnp.bfloat16)
                out_ref[2, low : low + size, :] = jnp.where(side, one[1], two[1]).astype(jnp.bfloat16)
        turned.append(total)
    both = jnp.transpose(jnp.concatenate(turned, 0)) * 0.125
    out_ref[0] = both.astype(jnp.bfloat16)


def attend_back(joined, mixed, grad, logsum):
    length, width = mixed.shape
    pairs, padded = width // LANES, round_up(length, LANES)
    block = lambda shift: pl.BlockSpec((padded, LANES), lambda i: (0, i + shift))
    return pl.pallas_call(
        functools.partial(attend_back_kernel, length),
        grid=(pairs,),
        in_specs=[
            block(0), block(pairs), block(2 * pairs), block(0), block(0),
            pl.BlockSpec((1, 2, padded), lambda i: (i, 0, 0)),
        ],
        out_specs=pl.BlockSpec((3, padded, LANES), lambda i: (0, 0, i)),
        out_shape=jax.ShapeDtypeStruct((3, length, width), jnp.bfloat16),
        compiler_params=pltpu.CompilerParams(vmem_limit_bytes=VMEM_LIMIT),
        cost_estimate=pl.CostEstimate(
            flops=40 * padded * padded * width, bytes_accessed=20 * length * width,
            transcendentals=padded * padded * 16,
        ),
        name="attend_back",
    )(joined, joined, joined, mixed, grad, logsum)


def dot(left, right, left_dim=1, right_dim=0):
    return contract(left, right, left_dim, right_dim)


def low(value):
    return value.astype(jnp.bfloat16)


def wide(value):
    return value.astype(jnp.float32)


def after(value, *others):
    return lax.optimization_barrier((value,) + others)[0]


def swap(value, axis):
    return lax.ppermute(value, axis, [(0, 1), (1, 0)])


def columns(value, start, size):
    return lax.dynamic_slice_in_dim(value, start, size, 1)


def rows(value, start, size):
    return lax.dynamic_slice_in_dim(value, start, size, 0)


def pair(own, other, second):
    return jnp.concatenate([jnp.where(second, other, own), jnp.where(second, own, other)])


def doubling(value, axis, size, keep):
    if size & (size - 1):
        return lax.psum(value, axis)
    step = 1
    while step < size:
        moved = lax.ppermute(value, axis, [(i, i ^ step) for i in range(size)])
        value = keep(wide(value) + wide(moved))
        step *= 2
    return value


def center(value):
    shifted = value - jnp.mean(value, -1, keepdims=True)
    inverse = lax.rsqrt(jnp.mean(shifted * shifted, -1, keepdims=True) + 1e-06)
    return shifted * inverse, inverse


def center_back(grad, gain, unit, inverse):
    scaled = grad * gain
    moved = scaled - jnp.mean(scaled, -1, keepdims=True)
    moved = moved - unit * jnp.mean(scaled * unit, -1, keepdims=True)
    return inverse * moved, jnp.sum(grad * unit, 0), jnp.sum(grad, 0)


def gather(weights, sizes):
    y_size = sizes["y"]
    if y_size != 2:
        return [lax.all_gather(w, "y", axis=0, tiled=True) for w in weights]
    here = {axis: lax.axis_index(axis) for axis in ("x", "c", "y")}
    fetched, gate = [], None
    for own in weights:
        size = own.shape[0] // 4
        block = rows(own, (here["c"] * 2 + here["x"]) * size, size)
        if gate is not None:
            block = after(block, gate)
        one = swap(block, "y")
        fetched.append(one)
        gate = one
    full = []
    for own, one in zip(weights, fetched):
        height, size = own.shape[0], own.shape[0] // 4
        two = swap(one, "x")
        far_one, far_two = swap(one, "c"), swap(two, "c")
        whole = jnp.zeros((2 * height, own.shape[1]), own.dtype)
        whole = lax.dynamic_update_slice(whole, own, (here["y"] * height, 0))
        for c_flip, x_flip, piece in ((0, 0, one), (0, 1, two), (1, 0, far_one), (1, 1, far_two)):
            spot = (here["c"] ^ c_flip) * 2 + (here["x"] ^ x_flip)
            whole = lax.dynamic_update_slice(
                whole, piece, ((1 - here["y"]) * height + spot * size, 0)
            )
        full.append(whole)
    return full


def reduce_weight(left, right, sizes, quick):
    here = {axis: lax.axis_index(axis) for axis in ("x", "c", "y")}
    y_size = sizes["y"]
    height = left.shape[1] // (2 * y_size)
    piece = lambda yi, ci: dot(columns(left, (yi * 2 + ci) * height, height), right, 0, 0)
    core, mine = here["c"], here["y"]
    if y_size == 2:
        far = swap(low(piece(1 - mine, 1 - core)), "c")
        sent = swap(low(piece(1 - mine, core) + wide(far)), "y")
        near = swap(low(piece(mine, 1 - core)), "c")
        kept = low(piece(mine, core) + wide(near) + wide(sent))
    else:
        moved = swap(jnp.stack([low(piece(i, 1 - core)) for i in range(y_size)]), "c")
        summed = jnp.stack([low(piece(i, core) + wide(moved[i])) for i in range(y_size)])
        kept = lax.psum_scatter(summed, "y", scatter_dimension=0, tiled=False)
    half = height // 2
    moved = swap(rows(kept, (1 - here["x"]) * half, half), "x")
    part = low(wide(rows(kept, here["x"] * half, half)) + wide(moved))
    if quick:
        part = doubling(part, "z", sizes["z"], low)
    else:
        part = lax.psum(part, "z")
    both = pair(part, swap(part, "x"), here["x"] == 1)
    return wide(pair(both, swap(both, "c"), core == 1))


def reduce_small(value, sizes):
    value = value.reshape(-1, LANES)
    for axis in ("c", "x", "z", "y"):
        value = doubling(value, axis, sizes[axis], wide)
    return value.reshape(-1)


def body(
    sizes,
    images,
    qkv_weight,
    out_weight,
    up_weight,
    down_weight,
    query_bias,
    value_bias,
    out_bias,
    up_bias,
    down_bias,
    first_gain,
    first_shift,
    second_gain,
    second_shift,
    cotangent,
):
    batch, length, width = images.shape
    vectors = (
        query_bias, value_bias, out_bias, up_bias, down_bias,
        first_gain, first_shift, second_gain, second_shift,
    )
    packed = lax.all_gather(jnp.concatenate(vectors), "y", axis=0, tiled=False)
    spread, start = [], 0
    for vector in vectors:
        spread.append(wide(packed[:, start : start + vector.shape[0]].reshape(-1)))
        start += vector.shape[0]
    (
        query_bias, value_bias, out_bias, up_bias, down_bias,
        first_gain, first_shift, second_gain, second_shift,
    ) = spread
    qkv_full, out_full, up_full, down_full = gather(
        [qkv_weight, out_weight, up_weight, down_weight], sizes
    )
    tokens = wide(images.reshape(batch * length, width))
    grad_out = cotangent.reshape(batch * length, width)
    unit_one, inverse_one = center(tokens)
    first = low(unit_one * first_gain + first_shift)
    joined_bias = jnp.concatenate([query_bias, jnp.zeros_like(query_bias), value_bias])
    joined = low(dot(first, qkv_full) + joined_bias)
    split = lambda value: [value[i * length : (i + 1) * length] for i in range(batch)]
    attended = [attend(item) for item in split(joined)]
    mixed = jnp.concatenate([item[0] for item in attended])
    resid = tokens + dot(mixed, out_full) + out_bias
    unit_two, inverse_two = center(resid)
    second = low(unit_two * second_gain + second_shift)
    hidden = dot(second, up_full) + up_bias
    below = 0.5 + 0.5 * lax.erf(hidden * (0.5**0.5))
    density = jnp.exp(-0.5 * hidden * hidden) * (1.0 / (2.0 * 3.141592653589793) ** 0.5)
    active, slope = lax.optimization_barrier((low(hidden * below), below + hidden * density))
    down_grad = reduce_weight(active, grad_out, sizes, False)
    down_bias_grad = jnp.sum(wide(grad_out), 0)
    grad_hidden = low(dot(grad_out, down_full, 1, 1) * slope)
    up_grad = reduce_weight(second, grad_hidden, sizes, False)
    up_bias_grad = jnp.sum(wide(grad_hidden), 0)
    grad_second = dot(grad_hidden, up_full, 1, 1)
    moved, second_gain_grad, second_shift_grad = center_back(
        grad_second, second_gain, unit_two, inverse_two
    )
    grad_resid = wide(grad_out) + moved
    grad_attn = low(grad_resid)
    out_grad = reduce_weight(mixed, grad_attn, sizes, False)
    out_bias_grad = jnp.sum(wide(grad_attn), 0)
    grad_mixed = low(dot(grad_attn, out_full, 1, 1))
    backs = [
        attend_back(item, own, grad, kept[1])
        for item, own, grad, kept in zip(split(joined), split(mixed), split(grad_mixed), attended)
    ]
    grad_joined = jnp.concatenate(
        [jnp.concatenate([back[i] for i in range(3)], -1) for back in backs]
    )
    qkv_grad = reduce_weight(first, grad_joined, sizes, True)
    bias_sums = jnp.sum(wide(grad_joined), 0)
    grad_first = dot(grad_joined, qkv_full, 1, 1)
    moved, first_gain_grad, first_shift_grad = center_back(
        grad_first, first_gain, unit_one, inverse_one
    )
    input_grad = grad_resid + moved
    output = low(resid + dot(active, down_full) + down_bias)
    small = (
        bias_sums[:width], bias_sums[2 * width :], out_bias_grad, up_bias_grad, down_bias_grad,
        first_gain_grad, first_shift_grad, second_gain_grad, second_shift_grad,
    )
    y_size, y_index = sizes["y"], lax.axis_index("y")
    summed = reduce_small(jnp.concatenate(small), sizes)
    owned, start = [], 0
    for vector in small:
        size = vector.shape[0] // y_size
        owned.append(lax.dynamic_slice_in_dim(summed, start + y_index * size, size))
        start += vector.shape[0]
    shape = (batch, length, width)
    return (
        output.reshape(shape), input_grad.reshape(shape),
        qkv_grad, out_grad, up_grad, down_grad, *owned,
    )


def solution(mesh):
    rep, shard = mesh.shape["rep"], mesh.shape["shard"]
    sizes = {"z": rep // 4, "x": 2, "c": 2, "y": shard}
    fine = Mesh(mesh.devices.reshape(tuple(sizes.values())), tuple(sizes))
    whole = P(("z", "x", "c", "y"), None, None)
    matrix, vector = P("y", None), P("y")
    return jax.shard_map(
        functools.partial(body, sizes),
        mesh=fine,
        in_specs=(whole,) + (matrix,) * 4 + (vector,) * 9 + (whole,),
        out_specs=(whole, whole) + (matrix,) * 4 + (vector,) * 9,
        check_vma=False,
    )
```

time: 1470 us -> 607 us (0.41)
  waiting for transfers between devices: 1040 us -> 303 us
  matrix products: 209 us -> 96.8 us
  blocking collectives: 110 us -> 15.2 us
  Pallas kernels: 0 us -> 46 us
  starting transfers between devices: 0.36 us -> 37.4 us
  local copies, waits for them, and re-layouts: 34.4 us -> 50.4 us
    reduce_scatter x4 -> x0, waiting for transfers between devices: 503 us -> none  [the longest x1 192 us: body(): lax.psum_scatter(up_local, 'shard', scatter_dimension=0, tiled=True)]
    psum x1, waiting for transfers between devices: 333 us -> 58.7 us  [reduce_weight(): part = lax.psum(part, 'z')]
    ppermute x0 -> x47, waiting for transfers between devices: none -> 245 us  [the longest x40 209 us: swap(): return lax.ppermute(value, axis, [(0, 1), (1, 0)])]
    all_gather x4 -> x0, waiting for transfers between devices: 205 us -> none  [the longest x1 84.5 us: body(): lax.all_gather(up_weight, 'shard', axis=0, tiled=True)]
    dot_general x18 -> x24, matrix products: 209 us -> 96.8 us  [contract(): lax.dot_general(left, right, (((left_dim,), (right_dim,)), ((), ())), pre...]
    psum x1 -> x0, blocking collectives: 62.4 us -> none  [body(): lax.psum((owned[0], owned[1], owned[2], owned[3], owned[4], owned[5], own...]
    pallas_call x0 -> x2, Pallas kernels: none -> 46 us  [the longest x1 30.5 us: attend_back(): pl.pallas_call(functools.partial(attend_back_kernel, length), grid=(pairs...]
    ppermute x0 -> x47, starting transfers between devices: none -> 37.4 us  [the longest x40 30.6 us: swap(): return lax.ppermute(value, axis, [(0, 1), (1, 0)])]
  transfers between devices with their start and end apart: 9 -> 48, of which waited for: 7 -> 14; matrix products, arithmetic and copies ran while one was open for 16% -> 28% of each run, Pallas kernels for 0% -> 8%
where the time goes in v1:
time: 607 us; the launch traced here: 600 us
  waiting for transfers between devices  303 us (50%)
  matrix products  96.8 us (16%)
  local copies, waits for them, and re-layouts  50.4 us (8%)
  Pallas kernels  46 us (8%)
  starting transfers between devices  37.4 us (6%)
  other arithmetic  34.8 us (6%)
  between operations  15.7 us (3%)
  blocking collectives  15.2 us (3%)
    ppermute x40, waiting for transfers between devices, swap(): return lax.ppermute(value, axis, [(0, 1), (1, 0)])  209 us
    dot_general x24, matrix products, contract(): lax.dot_general(left, right, (((left_dim,), (right_dim,)), ((), ())), pre...  96.8 us
    psum x1, waiting for transfers between devices, reduce_weight(): part = lax.psum(part, 'z')  58.7 us
    ppermute x7, waiting for transfers between devices, doubling(): moved = lax.ppermute(value, axis, [(i, i ^ step) for i in range(size)])  35.9 us
    ppermute x40, starting transfers between devices, swap(): return lax.ppermute(value, axis, [(0, 1), (1, 0)])  30.6 us
    pallas_call x1, Pallas kernels, attend_back(): pl.pallas_call(functools.partial(attend_back_kernel, length), grid=(pairs...  30.5 us
    pallas_call x1, Pallas kernels, attend(): pl.pallas_call(functools.partial(attend_kernel, length), grid=(pairs,), i...  15.5 us
    dynamic_update_slice x16, local copies, waits for them, and re-layouts, gather(): lax.dynamic_update_slice(whole, piece, ((1 - here['y']) * height + spot *...  15.5 us
  transfers between devices with their start and end apart: 48, of which 14 were waited for; matrix products, arithmetic and copies ran while one was open for 28% of the time, Pallas kernels for 8%

profile of v1, /device:TPU:0, one launch (start us, length us, event | category | flops | bytes accessed | tf_op | source)
XLA Modules:
  0.0 599.9 jit_solution(17794232933820416237)
XLA Ops:
  7.3 2.1 constant_dynamic-slice_fusion.7
  9.5 3.0 collective-permute-start
  15.3 15.2 %all-gather = bf16[12288]{0:T(1024)(128)(2,1)S(1)} all-gather(bf16[6144]{0:T(1024)(128)(2,1)S(1)} %dynamic-update-slice.17), channel_id=2, replica_groups=mesh['z'=4,'x'=2,'c'=2,'y'=2] {'y'}, dimensions={0}, use_global_device_ids=true | all-gather | bytes 36864 | tf_op jit(solution)/shard_map/all_gather | solution.py:299
  30.6 2.3 constant_dynamic-slice_fusion.5
  35.1 2.7 copy-done.5
  38.4 4.6 broadcast_in_dim.14
  43.0 2.5 constant_dynamic-update-slice_fusion.4
  46.1 4.4 broadcast_in_dim.13
  50.6 2.3 constant_dynamic-update-slice_fusion.9
  54.6 2.3 constant_dynamic-slice_fusion.4
  62.2 2.1 constant_dynamic-update-slice_fusion.18
  65.8 15.7 %collective-permute-done.5 = bf16[128,1024]{1,0:T(8,128)(2,1)S(1)} collective-permute-done((bf16[128,1024]{1,0:T(8,128)(2,1)}, bf16[128,1024]{1,0:T(8,128)(2,1)S(1)}, u32[]{:S(2)}, u32[]{:S(2)}) %collective-permute-start.5) | collective-permute-done | bytes 262176 | tf_op jit(solution)/shard_map/ppermute | solution.py:174
  85.0 4.5 collective-permute-done.8
  93.6 7.1 %add_convert_fusion.query_ref.key_ref.value_ref = bf16[577,3072]{1,0:T(8,128)(2,1)S(1)} fusion(bf16[577,1024]{1,0:T(8,128)(2,1)S(1)} %fusion.14, bf16[1024,3072]{1,0:T(8,128)(2,1)} %constant_dynamic-update-slice_fusion.15, f32[3072]{0:T(1024)S(1)} %pad_maximum_fusion.5), kind=kOutput, calls=%fused_computation.11 | convolution fusion | flops 3633715200 | bytes 11030528 | tf_op jit(solution)/shard_map/dot_general | solution.py:24
  100.7 15.5 %attend.1 = (bf16[577,1024]{1,0:T(8,128)(2,1)S(1)}, f32[8,2,640]{2,1,0:T(2,128)S(1)}) custom-call(bf16[577,3072]{1,0:T(8,128)(2,1)S(1)} %add_convert_fusion.query_ref.key_ref.value_ref, bf16[577,3072]{1,0:T(8,128)(2,1)S(1)} %add_convert_fusion.query_ref.key_ref.value_ref, bf16[577,3072]{1,0:T(8,128)(2,1)S(1)} %add_convert_fusion.query_ref.key_ref.value_ref), custom_call_target="tpu_custom_call" | custom-call | flops 6710886400 | bytes 4726784 | tf_op jit(solution)/shard_map/attend/pallas_call | solution.py:71
  121.5 2.3 constant_dynamic-update-slice_fusion.7
  125.9 12.7 %fusion.3 = (f32[577,4096]{1,0:T(8,128)}, bf16[577,4096]{1,0:T(8,128)(2,1)S(1)}) fusion(f32[4096]{0:T(1024)S(1)} %bitcast.134, bf16[577,1024]{1,0:T(8,128)(2,1)S(1)} %add_convert_fusion.8, bf16[1024,4096]{1,0:T(8,128)(2,1)} %constant_dynamic-update-slice_fusion.5), kind=kOutput, calls=%fused_computation.4 | convolution fusion | flops 4866224128 | bytes 23767040 | tf_op jit(solution)/shard_map/dot_general | solution.py:24
  138.6 5.7 collective-permute-done.13
  144.3 3.2 convolution_convert_fusion.4
  150.0 3.2 convolution_convert_fusion.5
  153.2 3.8 fusion.28
  158.1 10.3 %convert_reduce_fusion = (f32[4096]{0:T(1024)S(1)}, bf16[577,4096]{1,0:T(8,128)(2,1)S(1)}) fusion(f32[577,4096]{1,0:T(8,128)} %get-tuple-element.27, bf16[4096,1024]{1,0:T(8,128)(2,1)} %constant_dynamic-update-slice_fusion, bf16[1,577,1024]{2,1,0:T(8,128)(2,1)S(1)} %copy-done.11), kind=kOutput, calls=%fused_computation.7 | convolution fusion | flops 4849676288 | bytes 23767040 | tf_op jit(solution)/shard_map/dot_general | solution.py:24
  168.4 8.3 %multiply_reduce_fusion = (f32[1024]{0:T(1024)S(1)}, f32[577]{0:T(1024)S(1)}, f32[577]{0:T(1024)S(1)}, f32[1024]{0:T(1024)S(1)}, f32[577,1024]{1,0:T(8,128)S(1)}) fusion(f32[577,1024]{1,0:T(8,128)S(1)} %get-tuple-element.112, f32[577]{0:T(1024)S(1)} %add_rsqrt_fusion, f32[577]{0:T(1024)S(1)} %broadcast_multiply_fusion.4, f32[1024]{0:T(1024)S(1)} %bitcast.127, ...), kind=kOutput, calls=%fused_computation.48 | convolution fusion | flops 4845541376 | bytes 17863696 | tf_op jit(solution)/shard_map/dot_general | solution.py:24
  176.7 2.8 convert_reduce_fusion.4
  180.9 30.5 %attend_back.1 = bf16[3,577,1024]{2,1,0:T(8,128)(2,1)S(1)} custom-call(bf16[577,3072]{1,0:T(8,128)(2,1)} %copy-done, bf16[577,3072]{1,0:T(8,128)(2,1)} %copy-done, bf16[577,3072]{1,0:T(8,128)(2,1)} %copy-done, bf16[577,1024]{1,0:T(8,128)(2,1)S(1)} %get-tuple-element.22.mixed_ref, bf16[577,1024]{1,0:T(8,128)(2,1)S(1)} %convolution_convert_fusion.6.grad_ref, ...), custom_call_target="tpu_custom_call" | custom-call | flops 16777216000 | bytes 11816960 | tf_op jit(solution)/shard_map/attend_back/pallas_call | solution.py:139
  211.9 9.3 %fusion.20 = (f32[1024]{0:T(1024)S(1)}, f32[577]{0:T(1024)}, f32[577]{0:T(1024)}, f32[1024]{0:T(1024)S(1)}, f32[577,1024]{1,0:T(8,128)}) fusion(bf16[1,577,1024]{2,1,0:T(8,128)(2,1)S(1)} %copy-done.1, f32[577]{0:T(1024)S(1)} %add_rsqrt_fusion.1, f32[577]{0:T(1024)S(1)} %broadcast_multiply_fusion.5, f32[1024]{0:T(1024)S(1)} %bitcast.130, ...), kind=kOutput, calls=%fused_computation.45 | convolution fusion | flops 3646710784 | bytes 13403152 | tf_op jit(solution)/shard_map/dot_general | solution.py:24
  223.1 3.0 convolution_convert_fusion.2
  228.1 8.4 %fusion.23 = bf16[1,577,1024]{2,1,0:T(8,128)(2,1)} fusion(f32[577,1024]{1,0:T(8,128)S(1)} %get-tuple-element.112, bf16[577,4096]{1,0:T(8,128)(2,1)S(1)} %bitcast.140, bf16[4096,1024]{1,0:T(8,128)(2,1)} %constant_dynamic-update-slice_fusion, f32[1024]{0:T(1024)S(1)} %bitcast.137), kind=kOutput, calls=%fused_computation.74 | convolution fusion | flops 4841999360 | bytes 16664576 | tf_op jit(solution)/shard_map/dot_general | solution.py:24
  239.9 3.7 convolution_convert_fusion.3
  247.7 3.9 add_convert_fusion.6
  254.8 5.1 add_convert_fusion.2
  261.3 1.9 add_convert_fusion.4
  263.4 25.7 %collective-permute-done.18 = bf16[256,3072]{1,0:T(8,128)(2,1)S(1)} collective-permute-done((bf16[256,3072]{1,0:T(8,128)(2,1)}, bf16[256,3072]{1,0:T(8,128)(2,1)S(1)}, u32[]{:S(2)}, u32[]{:S(2)}) %collective-permute-start.18) | collective-permute-done | bytes 1572896 | tf_op jit(solution)/shard_map/ppermute | solution.py:174
  292.0 53.2 %collective-permute-done.26 = bf16[256,1024]{1,0:T(8,128)(2,1)S(1)} collective-permute-done((bf16[256,1024]{1,0:T(8,128)(2,1)S(1)}, bf16[256,1024]{1,0:T(8,128)(2,1)S(1)}, u32[]{:S(2)}, u32[]{:S(2)}) %collective-permute-start.26) | collective-permute-done | bytes 524320 | tf_op jit(solution)/shard_map/ppermute | solution.py:174
  350.5 15.2 %collective-permute-done.19 = bf16[128,3072]{1,0:T(8,128)(2,1)S(1)} collective-permute-done((bf16[128,3072]{1,0:T(8,128)(2,1)S(1)}, bf16[128,3072]{1,0:T(8,128)(2,1)S(1)}, u32[]{:S(2)}, u32[]{:S(2)}) %collective-permute-start.19) | collective-permute-done | bytes 786464 | tf_op jit(solution)/shard_map/ppermute | solution.py:174
  369.1 20.6 %collective-permute-done.32 = bf16[256,4096]{1,0:T(8,128)(2,1)S(1)} collective-permute-done((bf16[256,4096]{1,0:T(8,128)(2,1)S(1)}, bf16[256,4096]{1,0:T(8,128)(2,1)S(1)}, u32[]{:S(2)}, u32[]{:S(2)}) %collective-permute-start.32) | collective-permute-done | bytes 2097184 | tf_op jit(solution)/shard_map/ppermute | solution.py:174
  394.8 2.6 collective-permute-start.21
  397.4 18.2 %collective-permute-done.33 = bf16[128,4096]{1,0:T(8,128)(2,1)S(1)} collective-permute-done((bf16[128,4096]{1,0:T(8,128)(2,1)S(1)}, bf16[128,4096]{1,0:T(8,128)(2,1)S(1)}, u32[]{:S(2)}, u32[]{:S(2)}) %collective-permute-start.33) | collective-permute-done | bytes 1048608 | tf_op jit(solution)/shard_map/ppermute | solution.py:174
  418.6 11.7 %collective-permute-done.44 = f32[96,128]{1,0:T(8,128)S(1)} collective-permute-done((f32[96,128]{1,0:T(8,128)S(1)}, f32[96,128]{1,0:T(8,128)S(1)}, u32[]{:S(2)}, u32[]{:S(2)}) %collective-permute-start.44) | collective-permute-done | bytes 49184 | tf_op jit(solution)/shard_map/ppermute | solution.py:194
  430.4 24.2 %collective-permute-done.45 = f32[96,128]{1,0:T(8,128)S(1)} collective-permute-done((f32[96,128]{1,0:T(8,128)S(1)}, f32[96,128]{1,0:T(8,128)S(1)}, u32[]{:S(2)}, u32[]{:S(2)}) %collective-permute-start.45) | collective-permute-done | bytes 49184 | tf_op jit(solution)/shard_map/ppermute | solution.py:194
  455.0 2.5 fusion.19
  457.5 4.1 copy.31
  462.9 58.7 %all-reduce.3.cloned.1.call-done = (bf16[128,1024]{1,0:T(8,128)(2,1)}, bf16[128,4096]{1,0:T(8,128)(2,1)}, bf16[512,1024]{1,0:T(8,128)(2,1)}) async-done(((bf16[128,1024]{1,0:T(8,128)(2,1)}, bf16[128,4096]{1,0:T(8,128)(2,1)}, bf16[512,1024]{1,0:T(8,128)(2,1)}), (bf16[128,1024]{1,0:T(8,128)(2,1)}, bf16[128,4096]{1,0:T(8,128)(2,1)}, bf16[512,1024]{1,0:T(8,128)(2,1)})) %all-reduce.3.cloned.1.call-update) | async-done | bytes 2359312 | tf_op jit(solution)/shard_map/psum | solution.py:264
  525.4 28.0 %collective-permute-done.28 = bf16[128,1024]{1,0:T(8,128)(2,1)S(1)} collective-permute-done((bf16[128,1024]{1,0:T(8,128)(2,1)S(1)}, bf16[128,1024]{1,0:T(8,128)(2,1)S(1)}, u32[]{:S(2)}, u32[]{:S(2)}) %collective-permute-start.28) | collective-permute-done | bytes 262176 | tf_op jit(solution)/shard_map/ppermute | solution.py:174
  554.5 20.2 %collective-permute-done.34 = bf16[128,4096]{1,0:T(8,128)(2,1)S(1)} collective-permute-done((bf16[128,4096]{1,0:T(8,128)(2,1)S(1)}, bf16[128,4096]{1,0:T(8,128)(2,1)S(1)}, u32[]{:S(2)}, u32[]{:S(2)}) %collective-permute-start.34) | collective-permute-done | bytes 1048608 | tf_op jit(solution)/shard_map/ppermute | solution.py:174
  575.9 3.5 maximum_convert_fusion.2
  582.4 4.5 maximum_convert_fusion.1
  588.1 4.5 maximum_convert_fusion
  (280 shorter events, 82.5 us)
Async XLA Ops:
  7.3 514.3 %all-reduce.3.cloned.1.call-start = ((), (), s32[]{:S(2)}) async-start(), calls=%async_computation | async-start | bytes 4718592 | tf_op jit(solution)/shard_map/psum | solution.py:264
  9.5 43.4 %collective-permute-start = (bf16[128,3072]{1,0:T(8,128)(2,1)}, bf16[128,3072]{1,0:T(8,128)(2,1)}, u32[]{:S(2)}, u32[]{:S(2)}) collective-permute-start(bf16[128,3072]{1,0:T(8,128)(2,1)} %constant_dynamic-slice_fusion.7), channel_id=1, source_target_pairs={{0,1},{1,0},{2,3},{3,2},{4,5},{5,4},{6,7},{7,6},{8,9},{9,8},{10,11... | collective-permute-start | bytes 2359304 | tf_op jit(solution)/shard_map/ppermute | solution.py:174
  52.9 7.9 %collective-permute-start.4 = (bf16[128,1024]{1,0:T(8,128)(2,1)}, bf16[128,1024]{1,0:T(8,128)(2,1)}, u32[]{:S(2)}, u32[]{:S(2)}) collective-permute-start(bf16[128,1024]{1,0:T(8,128)(2,1)} %constant_dynamic-slice_fusion.6), channel_id=1, source_target_pairs={{0,1},{1,0},{2,3},{3,2},{4,5},{5,4},{6,7},{7,6},{8,9},{9,8},{10,11... | collective-permute-start | bytes 786440 | tf_op jit(solution)/shard_map/ppermute | solution.py:174
  57.4 25.2 %collective-permute-start.1 = (bf16[128,3072]{1,0:T(8,128)(2,1)}, bf16[128,3072]{1,0:T(8,128)(2,1)S(1)}, u32[]{:S(2)}, u32[]{:S(2)}) collective-permute-start(bf16[128,3072]{1,0:T(8,128)(2,1)} %collective-permute-done), channel_id=1, source_target_pairs={{0,4},{4,0},{1,5},{5,1},{2,6},{6,2},{3,7},{7,3},{8,12},{12,8},{9,1... | collective-permute-start | bytes 2359304 | tf_op jit(solution)/shard_map/ppermute | solution.py:174
  58.9 25.2 %collective-permute-start.2 = (bf16[128,3072]{1,0:T(8,128)(2,1)}, bf16[128,3072]{1,0:T(8,128)(2,1)S(1)}, u32[]{:S(2)}, u32[]{:S(2)}) collective-permute-start(bf16[128,3072]{1,0:T(8,128)(2,1)} %collective-permute-done), channel_id=1, source_target_pairs={{0,2},{2,0},{1,3},{3,1},{4,6},{6,4},{5,7},{7,5},{8,10},{10,8},{9,1... | collective-permute-start | bytes 2359304 | tf_op jit(solution)/shard_map/ppermute | solution.py:174
  60.8 21.7 %collective-permute-start.6 = (bf16[128,1024]{1,0:T(8,128)(2,1)}, bf16[128,1024]{1,0:T(8,128)(2,1)S(1)}, u32[]{:S(2)}, u32[]{:S(2)}) collective-permute-start(bf16[128,1024]{1,0:T(8,128)(2,1)} %collective-permute-done.4), channel_id=1, source_target_pairs={{0,2},{2,0},{1,3},{3,1},{4,6},{6,4},{5,7},{7,5},{8,10},{10,8},{9,1... | collective-permute-start | bytes 786440 | tf_op jit(solution)/shard_map/ppermute | solution.py:174
  60.8 20.7 %collective-permute-start.5 = (bf16[128,1024]{1,0:T(8,128)(2,1)}, bf16[128,1024]{1,0:T(8,128)(2,1)S(1)}, u32[]{:S(2)}, u32[]{:S(2)}) collective-permute-start(bf16[128,1024]{1,0:T(8,128)(2,1)} %collective-permute-done.4), channel_id=1, source_target_pairs={{0,4},{4,0},{1,5},{5,1},{2,6},{6,2},{3,7},{7,3},{8,12},{12,8},{9,1... | collective-permute-start | bytes 786440 | tf_op jit(solution)/shard_map/ppermute | solution.py:174
  64.2 25.3 %collective-permute-start.8 = (bf16[128,4096]{1,0:T(8,128)(2,1)S(1)}, bf16[128,4096]{1,0:T(8,128)(2,1)S(1)}, u32[]{:S(2)}, u32[]{:S(2)}) collective-permute-start(bf16[128,4096]{1,0:T(8,128)(2,1)S(1)} %copy-done.18), channel_id=1, source_target_pairs={{0,1},{1,0},{2,3},{3,2},{4,5},{5,4},{6,7},{7,6},{8,9},{9,8},{10,11... | collective-permute-start | bytes 3145736 | tf_op jit(solution)/shard_map/ppermute | solution.py:174
  81.5 1.6 collective-permute-start.7
  82.5 10.1 %collective-permute-start.3 = (bf16[128,3072]{1,0:T(8,128)(2,1)S(1)}, bf16[128,3072]{1,0:T(8,128)(2,1)S(1)}, u32[]{:S(2)}, u32[]{:S(2)}) collective-permute-start(bf16[128,3072]{1,0:T(8,128)(2,1)S(1)} %collective-permute-done.1), channel_id=1, source_target_pairs={{0,2},{2,0},{1,3},{3,1},{4,6},{6,4},{5,7},{7,5},{8,10},{10,8},{9,1... | collective-permute-start | bytes 2359304 | tf_op jit(solution)/shard_map/ppermute | solution.py:174
  89.5 29.1 %collective-permute-start.12 = (bf16[512,1024]{1,0:T(8,128)(2,1)S(1)}, bf16[512,1024]{1,0:T(8,128)(2,1)S(1)}, u32[]{:S(2)}, u32[]{:S(2)}) collective-permute-start(bf16[512,1024]{1,0:T(8,128)(2,1)S(1)} %copy-done.17), channel_id=1, source_target_pairs={{0,1},{1,0},{2,3},{3,2},{4,5},{5,4},{6,7},{7,6},{8,9},{9,8},{10,11... | collective-permute-start | bytes 3145736 | tf_op jit(solution)/shard_map/ppermute | solution.py:174
  91.1 32.7 %collective-permute-start.10 = (bf16[128,4096]{1,0:T(8,128)(2,1)S(1)}, bf16[128,4096]{1,0:T(8,128)(2,1)S(1)}, u32[]{:S(2)}, u32[]{:S(2)}) collective-permute-start(bf16[128,4096]{1,0:T(8,128)(2,1)S(1)} %collective-permute-done.8), channel_id=1, source_target_pairs={{0,2},{2,0},{1,3},{3,1},{4,6},{6,4},{5,7},{7,5},{8,10},{10,8},{9,1... | collective-permute-start | bytes 3145736 | tf_op jit(solution)/shard_map/ppermute | solution.py:174
  91.1 29.4 %collective-permute-start.9 = (bf16[128,4096]{1,0:T(8,128)(2,1)S(1)}, bf16[128,4096]{1,0:T(8,128)(2,1)}, u32[]{:S(2)}, u32[]{:S(2)}) collective-permute-start(bf16[128,4096]{1,0:T(8,128)(2,1)S(1)} %collective-permute-done.8), channel_id=1, source_target_pairs={{0,4},{4,0},{1,5},{5,1},{2,6},{6,2},{3,7},{7,3},{8,12},{12,8},{9,1... | collective-permute-start | bytes 3145736 | tf_op jit(solution)/shard_map/ppermute | solution.py:174
  118.6 30.4 %collective-permute-start.14 = (bf16[512,1024]{1,0:T(8,128)(2,1)S(1)}, bf16[512,1024]{1,0:T(8,128)(2,1)S(1)}, u32[]{:S(2)}, u32[]{:S(2)}) collective-permute-start(bf16[512,1024]{1,0:T(8,128)(2,1)S(1)} %collective-permute-done.12), channel_id=1, source_target_pairs={{0,2},{2,0},{1,3},{3,1},{4,6},{6,4},{5,7},{7,5},{8,10},{10,8},{9,1... | collective-permute-start | bytes 3145736 | tf_op jit(solution)/shard_map/ppermute | solution.py:174
  118.9 25.3 %collective-permute-start.13 = (bf16[512,1024]{1,0:T(8,128)(2,1)S(1)}, bf16[512,1024]{1,0:T(8,128)(2,1)S(1)}, u32[]{:S(2)}, u32[]{:S(2)}) collective-permute-start(bf16[512,1024]{1,0:T(8,128)(2,1)S(1)} %collective-permute-done.12), channel_id=1, source_target_pairs={{0,4},{4,0},{1,5},{5,1},{2,6},{6,2},{3,7},{7,3},{8,12},{12,8},{9,1... | collective-permute-start | bytes 3145736 | tf_op jit(solution)/shard_map/ppermute | solution.py:174
  120.4 4.4 collective-permute-start.11
  144.3 12.8 %collective-permute-start.15 = (bf16[512,1024]{1,0:T(8,128)(2,1)S(1)}, bf16[512,1024]{1,0:T(8,128)(2,1)S(1)}, u32[]{:S(2)}, u32[]{:S(2)}) collective-permute-start(bf16[512,1024]{1,0:T(8,128)(2,1)S(1)} %collective-permute-done.13), channel_id=1, source_target_pairs={{0,2},{2,0},{1,3},{3,1},{4,6},{6,4},{5,7},{7,5},{8,10},{10,8},{9,1... | collective-permute-start | bytes 3145736 | tf_op jit(solution)/shard_map/ppermute | solution.py:174
  147.4 106.9 %collective-permute-start.37 = (bf16[1024,1024]{1,0:T(8,128)(2,1)}, bf16[1024,1024]{1,0:T(8,128)(2,1)}, u32[]{:S(2)}, u32[]{:S(2)}) collective-permute-start(bf16[1024,1024]{1,0:T(8,128)(2,1)} %convolution_convert_fusion.4), channel_id=1, source_target_pairs={{0,2},{2,0},{1,3},{3,1},{4,6},{6,4},{5,7},{7,5},{8,10},{10,8},{9,1... | collective-permute-start | bytes 6291464 | tf_op jit(solution)/shard_map/ppermute | solution.py:174
  236.6 15.0 %collective-permute-start.42 = (f32[96,128]{1,0:T(8,128)S(1)}, f32[96,128]{1,0:T(8,128)S(1)}, u32[]{:S(2)}, u32[]{:S(2)}) collective-permute-start(f32[96,128]{1,0:T(8,128)S(1)} %bitcast.125), channel_id=1, source_target_pairs={{0,2},{2,0},{1,3},{3,1},{4,6},{6,4},{5,7},{7,5},{8,10},{10,8},{9,1... | collective-permute-start | bytes 147464 | tf_op jit(solution)/shard_map/ppermute | solution.py:194
  236.6 16.9 %collective-permute-start.25 = (bf16[256,1024]{1,0:T(8,128)(2,1)S(1)}, bf16[256,1024]{1,0:T(8,128)(2,1)S(1)}, u32[]{:S(2)}, u32[]{:S(2)}) collective-permute-start(bf16[256,1024]{1,0:T(8,128)(2,1)S(1)} %convolution_convert_fusion.7), channel_id=1, source_target_pairs={{0,2},{2,0},{1,3},{3,1},{4,6},{6,4},{5,7},{7,5},{8,10},{10,8},{9,1... | collective-permute-start | bytes 1572872 | tf_op jit(solution)/shard_map/ppermute | solution.py:174
  237.1 10.4 %collective-permute-start.17 = (bf16[256,3072]{1,0:T(8,128)(2,1)S(1)}, bf16[256,3072]{1,0:T(8,128)(2,1)S(1)}, u32[]{:S(2)}, u32[]{:S(2)}) collective-permute-start(bf16[256,3072]{1,0:T(8,128)(2,1)S(1)} %convolution_convert_fusion.2), channel_id=1, source_target_pairs={{0,2},{2,0},{1,3},{3,1},{4,6},{6,4},{5,7},{7,5},{8,10},{10,8},{9,1... | collective-permute-start | bytes 4718600 | tf_op jit(solution)/shard_map/ppermute | solution.py:174
  237.9 22.0 %collective-permute-start.31 = (bf16[256,4096]{1,0:T(8,128)(2,1)S(1)}, bf16[256,4096]{1,0:T(8,128)(2,1)S(1)}, u32[]{:S(2)}, u32[]{:S(2)}) collective-permute-start(bf16[256,4096]{1,0:T(8,128)(2,1)S(1)} %convolution_convert_fusion), channel_id=1, source_target_pairs={{0,2},{2,0},{1,3},{3,1},{4,6},{6,4},{5,7},{7,5},{8,10},{10,8},{9,1... | collective-permute-start | bytes 6291464 | tf_op jit(solution)/shard_map/ppermute | solution.py:174
  247.5 15.8 %collective-permute-start.16 = (bf16[256,3072]{1,0:T(8,128)(2,1)}, bf16[256,3072]{1,0:T(8,128)(2,1)S(1)}, u32[]{:S(2)}, u32[]{:S(2)}) collective-permute-start(bf16[256,3072]{1,0:T(8,128)(2,1)} %convolution_convert_fusion.3), channel_id=1, source_target_pairs={{0,2},{2,0},{1,3},{3,1},{4,6},{6,4},{5,7},{7,5},{8,10},{10,8},{9,1... | collective-permute-start | bytes 4718600 | tf_op jit(solution)/shard_map/ppermute | solution.py:174
  251.6 37.5 %collective-permute-start.18 = (bf16[256,3072]{1,0:T(8,128)(2,1)}, bf16[256,3072]{1,0:T(8,128)(2,1)S(1)}, u32[]{:S(2)}, u32[]{:S(2)}) collective-permute-start(bf16[256,3072]{1,0:T(8,128)(2,1)} %add_convert_fusion.6), channel_id=1, source_target_pairs={{0,1},{1,0},{2,3},{3,2},{4,5},{5,4},{6,7},{7,6},{8,9},{9,8},{10,11... | collective-permute-start | bytes 4718600 | tf_op jit(solution)/shard_map/ppermute | solution.py:174
  253.5 93.5 %collective-permute-start.36 = (bf16[1024,1024]{1,0:T(8,128)(2,1)}, bf16[1024,1024]{1,0:T(8,128)(2,1)S(1)}, u32[]{:S(2)}, u32[]{:S(2)}) collective-permute-start(bf16[1024,1024]{1,0:T(8,128)(2,1)} %convolution_convert_fusion.5), channel_id=1, source_target_pairs={{0,2},{2,0},{1,3},{3,1},{4,6},{6,4},{5,7},{7,5},{8,10},{10,8},{9,1... | collective-permute-start | bytes 6291464 | tf_op jit(solution)/shard_map/ppermute | solution.py:174
  254.4 36.1 %collective-permute-start.24 = (bf16[256,1024]{1,0:T(8,128)(2,1)S(1)}, bf16[256,1024]{1,0:T(8,128)(2,1)S(1)}, u32[]{:S(2)}, u32[]{:S(2)}) collective-permute-start(bf16[256,1024]{1,0:T(8,128)(2,1)S(1)} %convolution_convert_fusion.8), channel_id=1, source_target_pairs={{0,2},{2,0},{1,3},{3,1},{4,6},{6,4},{5,7},{7,5},{8,10},{10,8},{9,1... | collective-permute-start | bytes 1572872 | tf_op jit(solution)/shard_map/ppermute | solution.py:174
  259.9 87.7 %collective-permute-start.38 = (bf16[1024,1024]{1,0:T(8,128)(2,1)}, bf16[1024,1024]{1,0:T(8,128)(2,1)S(1)}, u32[]{:S(2)}, u32[]{:S(2)}) collective-permute-start(bf16[1024,1024]{1,0:T(8,128)(2,1)} %add_convert_fusion.2), channel_id=1, source_target_pairs={{0,1},{1,0},{2,3},{3,2},{4,5},{5,4},{6,7},{7,6},{8,9},{9,8},{10,11... | collective-permute-start | bytes 6291464 | tf_op jit(solution)/shard_map/ppermute | solution.py:174
  263.3 104.1 %collective-permute-start.30 = (bf16[256,4096]{1,0:T(8,128)(2,1)S(1)}, bf16[256,4096]{1,0:T(8,128)(2,1)S(1)}, u32[]{:S(2)}, u32[]{:S(2)}) collective-permute-start(bf16[256,4096]{1,0:T(8,128)(2,1)S(1)} %convolution_convert_fusion.1), channel_id=1, source_target_pairs={{0,2},{2,0},{1,3},{3,1},{4,6},{6,4},{5,7},{7,5},{8,10},{10,8},{9,1... | collective-permute-start | bytes 6291464 | tf_op jit(solution)/shard_map/ppermute | solution.py:174
  289.0 56.2 %collective-permute-start.26 = (bf16[256,1024]{1,0:T(8,128)(2,1)S(1)}, bf16[256,1024]{1,0:T(8,128)(2,1)S(1)}, u32[]{:S(2)}, u32[]{:S(2)}) collective-permute-start(bf16[256,1024]{1,0:T(8,128)(2,1)S(1)} %add_convert_fusion.15), channel_id=1, source_target_pairs={{0,1},{1,0},{2,3},{3,2},{4,5},{5,4},{6,7},{7,6},{8,9},{9,8},{10,11... | collective-permute-start | bytes 1572872 | tf_op jit(solution)/shard_map/ppermute | solution.py:174
  290.4 99.2 %collective-permute-start.32 = (bf16[256,4096]{1,0:T(8,128)(2,1)S(1)}, bf16[256,4096]{1,0:T(8,128)(2,1)S(1)}, u32[]{:S(2)}, u32[]{:S(2)}) collective-permute-start(bf16[256,4096]{1,0:T(8,128)(2,1)S(1)} %add_convert_fusion.4), channel_id=1, source_target_pairs={{0,1},{1,0},{2,3},{3,2},{4,5},{5,4},{6,7},{7,6},{8,9},{9,8},{10,11... | collective-permute-start | bytes 6291464 | tf_op jit(solution)/shard_map/ppermute | solution.py:174
  345.2 20.5 %collective-permute-start.19 = (bf16[128,3072]{1,0:T(8,128)(2,1)S(1)}, bf16[128,3072]{1,0:T(8,128)(2,1)S(1)}, u32[]{:S(2)}, u32[]{:S(2)}) collective-permute-start(bf16[128,3072]{1,0:T(8,128)(2,1)S(1)} %constant_dynamic-slice_fusion.3), channel_id=1, source_target_pairs={{0,4},{4,0},{1,5},{5,1},{2,6},{6,2},{3,7},{7,3},{8,12},{12,8},{9,1... | collective-permute-start | bytes 2359304 | tf_op jit(solution)/shard_map/ppermute | solution.py:174
  347.0 69.8 %collective-permute-start.43 = (f32[96,128]{1,0:T(8,128)}, f32[96,128]{1,0:T(8,128)S(1)}, u32[]{:S(2)}, u32[]{:S(2)}) collective-permute-start(f32[96,128]{1,0:T(8,128)} %bitcast_add_fusion), channel_id=1, source_target_pairs={{0,4},{4,0},{1,5},{5,1},{2,6},{6,2},{3,7},{7,3},{8,12},{12,8},{9,1... | collective-permute-start | bytes 147464 | tf_op jit(solution)/shard_map/ppermute | solution.py:194
  347.6 44.7 %collective-permute-start.27 = (bf16[128,1024]{1,0:T(8,128)(2,1)S(1)}, bf16[128,1024]{1,0:T(8,128)(2,1)S(1)}, u32[]{:S(2)}, u32[]{:S(2)}) collective-permute-start(bf16[128,1024]{1,0:T(8,128)(2,1)S(1)} %constant_dynamic-slice_fusion.2), channel_id=1, source_target_pairs={{0,4},{4,0},{1,5},{5,1},{2,6},{6,2},{3,7},{7,3},{8,12},{12,8},{9,1... | collective-permute-start | bytes 786440 | tf_op jit(solution)/shard_map/ppermute | solution.py:174
  365.7 27.5 %collective-permute-start.39 = (bf16[512,1024]{1,0:T(8,128)(2,1)S(1)}, bf16[512,1024]{1,0:T(8,128)(2,1)S(1)}, u32[]{:S(2)}, u32[]{:S(2)}) collective-permute-start(bf16[512,1024]{1,0:T(8,128)(2,1)S(1)} %constant_dynamic-slice_fusion), channel_id=1, source_target_pairs={{0,4},{4,0},{1,5},{5,1},{2,6},{6,2},{3,7},{7,3},{8,12},{12,8},{9,1... | collective-permute-start | bytes 3145736 | tf_op jit(solution)/shard_map/ppermute | solution.py:174
  367.4 27.1 %collective-permute-start.20 = (bf16[128,3072]{1,0:T(8,128)(2,1)S(1)}, bf16[128,3072]{1,0:T(8,128)(2,1)S(1)}, u32[]{:S(2)}, u32[]{:S(2)}) collective-permute-start(bf16[128,3072]{1,0:T(8,128)(2,1)S(1)} %add_convert_fusion.13), channel_id=1, source_target_pairs={{0,8},{8,0},{16,24},{24,16},{1,9},{9,1},{17,25},{25,17},{2,10},{10... | collective-permute-start | bytes 2359304 | tf_op jit(solution)/shard_map/ppermute | solution.py:194
  390.8 24.8 %collective-permute-start.33 = (bf16[128,4096]{1,0:T(8,128)(2,1)S(1)}, bf16[128,4096]{1,0:T(8,128)(2,1)S(1)}, u32[]{:S(2)}, u32[]{:S(2)}) collective-permute-start(bf16[128,4096]{1,0:T(8,128)(2,1)S(1)} %constant_dynamic-slice_fusion.1), channel_id=1, source_target_pairs={{0,4},{4,0},{1,5},{5,1},{2,6},{6,2},{3,7},{7,3},{8,12},{12,8},{9,1... | collective-permute-start | bytes 3145736 | tf_op jit(solution)/shard_map/ppermute | solution.py:174
  394.8 59.9 %collective-permute-start.21 = (bf16[128,3072]{1,0:T(8,128)(2,1)S(1)}, bf16[128,3072]{1,0:T(8,128)(2,1)S(1)}, u32[]{:S(2)}, u32[]{:S(2)}) collective-permute-start(bf16[128,3072]{1,0:T(8,128)(2,1)S(1)} %add_convert_fusion.12), channel_id=1, source_target_pairs={{0,16},{8,24},{16,0},{24,8},{1,17},{9,25},{17,1},{25,9},{2,18},{10... | collective-permute-start | bytes 2359304 | tf_op jit(solution)/shard_map/ppermute | solution.py:194
  416.9 13.4 %collective-permute-start.44 = (f32[96,128]{1,0:T(8,128)S(1)}, f32[96,128]{1,0:T(8,128)S(1)}, u32[]{:S(2)}, u32[]{:S(2)}) collective-permute-start(f32[96,128]{1,0:T(8,128)S(1)} %fusion.102), channel_id=1, source_target_pairs={{0,8},{8,0},{16,24},{24,16},{1,9},{9,1},{17,25},{25,17},{2,10},{10... | collective-permute-start | bytes 147464 | tf_op jit(solution)/shard_map/ppermute | solution.py:194
  430.3 24.3 %collective-permute-start.45 = (f32[96,128]{1,0:T(8,128)S(1)}, f32[96,128]{1,0:T(8,128)S(1)}, u32[]{:S(2)}, u32[]{:S(2)}) collective-permute-start(f32[96,128]{1,0:T(8,128)S(1)} %add.464), channel_id=1, source_target_pairs={{0,16},{8,24},{16,0},{24,8},{1,17},{9,25},{17,1},{25,9},{2,18},{10... | collective-permute-start | bytes 147464 | tf_op jit(solution)/shard_map/ppermute | solution.py:194
  454.6 7.0 %collective-permute-start.46 = (f32[96,128]{1,0:T(8,128)S(1)}, f32[96,128]{1,0:T(8,128)S(1)}, u32[]{:S(2)}, u32[]{:S(2)}) collective-permute-start(f32[96,128]{1,0:T(8,128)S(1)} %add.465), channel_id=1, source_target_pairs={{0,1},{1,0},{2,3},{3,2},{4,5},{5,4},{6,7},{7,6},{8,9},{9,8},{10,11... | collective-permute-start | bytes 147464 | tf_op jit(solution)/shard_map/ppermute | solution.py:194
  454.9 68.2 %collective-permute-start.22 = (bf16[128,3072]{1,0:T(8,128)(2,1)S(1)}, bf16[128,3072]{1,0:T(8,128)(2,1)S(1)}, u32[]{:S(2)}, u32[]{:S(2)}) collective-permute-start(bf16[128,3072]{1,0:T(8,128)(2,1)S(1)} %add_convert_fusion.11), channel_id=1, source_target_pairs={{0,4},{4,0},{1,5},{5,1},{2,6},{6,2},{3,7},{7,3},{8,12},{12,8},{9,1... | collective-permute-start | bytes 2359304 | tf_op jit(solution)/shard_map/ppermute | solution.py:174
  521.5 32.1 %collective-permute-start.40 = (bf16[512,1024]{1,0:T(8,128)(2,1)}, bf16[512,1024]{1,0:T(8,128)(2,1)S(1)}, u32[]{:S(2)}, u32[]{:S(2)}) collective-permute-start(bf16[512,1024]{1,0:T(8,128)(2,1)} %get-tuple-element.69), channel_id=1, source_target_pairs={{0,4},{4,0},{1,5},{5,1},{2,6},{6,2},{3,7},{7,3},{8,12},{12,8},{9,1... | collective-permute-start | bytes 3145736 | tf_op jit(solution)/shard_map/ppermute | solution.py:174
  523.1 30.3 %collective-permute-start.28 = (bf16[128,1024]{1,0:T(8,128)(2,1)S(1)}, bf16[128,1024]{1,0:T(8,128)(2,1)S(1)}, u32[]{:S(2)}, u32[]{:S(2)}) collective-permute-start(bf16[128,1024]{1,0:T(8,128)(2,1)S(1)} %copy-done.19), channel_id=1, source_target_pairs={{0,4},{4,0},{1,5},{5,1},{2,6},{6,2},{3,7},{7,3},{8,12},{12,8},{9,1... | collective-permute-start | bytes 786440 | tf_op jit(solution)/shard_map/ppermute | solution.py:174
  524.0 50.8 %collective-permute-start.34 = (bf16[128,4096]{1,0:T(8,128)(2,1)S(1)}, bf16[128,4096]{1,0:T(8,128)(2,1)S(1)}, u32[]{:S(2)}, u32[]{:S(2)}) collective-permute-start(bf16[128,4096]{1,0:T(8,128)(2,1)S(1)} %copy-done.15), channel_id=1, source_target_pairs={{0,4},{4,0},{1,5},{5,1},{2,6},{6,2},{3,7},{7,3},{8,12},{12,8},{9,1... | collective-permute-start | bytes 3145736 | tf_op jit(solution)/shard_map/ppermute | solution.py:174
  525.3 49.9 %collective-permute-start.23 = (bf16[256,3072]{1,0:T(8,128)(2,1)S(1)}, bf16[256,3072]{1,0:T(8,128)(2,1)S(1)}, u32[]{:S(2)}, u32[]{:S(2)}) collective-permute-start(bf16[256,3072]{1,0:T(8,128)(2,1)S(1)} %pad_maximum_fusion.3), channel_id=1, source_target_pairs={{0,2},{2,0},{1,3},{3,1},{4,6},{6,4},{5,7},{7,5},{8,10},{10,8},{9,1... | collective-permute-start | bytes 4718600 | tf_op jit(solution)/shard_map/ppermute | solution.py:174
  553.5 25.9 %collective-permute-start.29 = (bf16[256,1024]{1,0:T(8,128)(2,1)S(1)}, bf16[256,1024]{1,0:T(8,128)(2,1)S(1)}, u32[]{:S(2)}, u32[]{:S(2)}) collective-permute-start(bf16[256,1024]{1,0:T(8,128)(2,1)S(1)} %pad_maximum_fusion.4), channel_id=1, source_target_pairs={{0,2},{2,0},{1,3},{3,1},{4,6},{6,4},{5,7},{7,5},{8,10},{10,8},{9,1... | collective-permute-start | bytes 1572872 | tf_op jit(solution)/shard_map/ppermute | solution.py:174
  553.9 27.3 %collective-permute-start.41 = (bf16[1024,1024]{1,0:T(8,128)(2,1)S(1)}, bf16[1024,1024]{1,0:T(8,128)(2,1)S(1)}, u32[]{:S(2)}, u32[]{:S(2)}) collective-permute-start(bf16[1024,1024]{1,0:T(8,128)(2,1)S(1)} %pad_maximum_fusion.2), channel_id=1, source_target_pairs={{0,2},{2,0},{1,3},{3,1},{4,6},{6,4},{5,7},{7,5},{8,10},{10,8},{9,1... | collective-permute-start | bytes 6291464 | tf_op jit(solution)/shard_map/ppermute | solution.py:174
  575.2 11.7 %collective-permute-start.35 = (bf16[256,4096]{1,0:T(8,128)(2,1)S(1)}, bf16[256,4096]{1,0:T(8,128)(2,1)S(1)}, u32[]{:S(2)}, u32[]{:S(2)}) collective-permute-start(bf16[256,4096]{1,0:T(8,128)(2,1)S(1)} %pad_maximum_fusion.1), channel_id=1, source_target_pairs={{0,2},{2,0},{1,3},{3,1},{4,6},{6,4},{5,7},{7,5},{8,10},{10,8},{9,1... | collective-permute-start | bytes 6291464 | tf_op jit(solution)/shard_map/ppermute | solution.py:174
  (44 other events, 1172.7 us)
Sparse Core Ops, SparseCore 0:
  416.9 104.5 all-reduce.2
